TPU v7x, 32 devices: a whole 2x2x4 slice. The times are simulated.
32 devices in a mesh: rows: 8 (over z, y), vec: 4 (over x, core).
Axes of the slice: x: 2, y: 2, z: 4, core: 2. Of those that a mesh axis runs over, the one named last changes fastest.
Arguments:
- self_tiles: bfloat16 [64, 256, 256], P('rows'), may hold values from 0.01 to 1, as said below
- link_tiles: bfloat16 [64, 3, 256, 256], P('rows'), may hold values from 0.01 to 1, as said below
- links: int32 [64, 3], replicated, may hold values from 0 to 63, as said below
- coarse_row: int32 [64], replicated, may hold values from 0 to 31, as said below
- vectors: float32 [16, 16384], P('vec', 'rows'), may hold values from -70 to 70
- directions: float32 [16, 16384], P('vec', 'rows'), may hold values from -70 to 70
Outputs:
- residual: float32 [16, 16384], P('vec', 'rows')
- corrected: float32 [16, 16384], P('vec', 'rows')
- projected: float32 [48, 48], replicated
Inputs may be any that keep to these rules, and one draw needn't show every extreme that they name: For each slot s, links[., s] pairs the row blocks: links[links[b, s], s] = b and links[b, s] != b; the linked block lies on the same slab of 8 blocks as b or on the slab just before or after it (blocks numbered slab by slab). `coarse_row`: each coarse row numbers exactly two row blocks. `self_tiles`: each tile is symmetric, entries positive. link_tiles[b, s] is the transpose of link_tiles[links[b, s], s]; entries positive.
All inputs are finite; a program needn't handle non-finite values.
Results may differ from a plain program's by a relative error of at most 0.0029.
Values may be sent and summed in bfloat16 or wider, within the bound.
A program may use at most 128 MiB of HBM per device.

v0:
```python
import functools

import jax
import jax.numpy as jnp
from jax import lax
from jax.experimental import pallas as pl
from jax.experimental.pallas import tpu as pltpu
from jax.sharding import PartitionSpec as P

spectral_shift = 0.25
damping = 0.6
MESH = pl.DeviceIdType.MESH
F32 = jnp.float32

EX_GRAM_X, EX_CROSS, EX_RHS, EX_GRAM_B, EX_GRAM_A = range(5)
EX_XP, EX_W, EX_FINAL = range(3)


def dot_nt(a, b):
    return lax.dot_general(
        a, b, (((1,), (1,)), ((), ())), precision=lax.Precision.HIGHEST, preferred_element_type=F32
    )


def dot_nn(a, b):
    return lax.dot_general(
        a, b, (((1,), (0,)), ((), ())), precision=lax.Precision.HIGHEST, preferred_element_type=F32
    )


def tile_dot(tile, rows):
    return lax.dot_general(tile, rows, (((1,), (1,)), ((), ())), preferred_element_type=F32)


def in_slot(rows, b, count):
    zero = jnp.zeros((8, rows.shape[1]), F32)
    if rows.shape[0] < 8:
        rows = jnp.concatenate([rows, zero[rows.shape[0] :]], axis=0)
    parts = [zero] * b + [rows] + [zero] * (count - 1 - b)
    return jnp.concatenate(parts, axis=0).astype(jnp.bfloat16)


def iota(shape, axis):
    return lax.broadcasted_iota(jnp.int32, shape, axis)


def eliminate(both, n, below_only):
    width = both.shape[1]
    sub = iota((n, width), 0)
    group = 4 if n % 4 == 0 else 1
    for k in range(0, n, group):
        cols = [jnp.broadcast_to(both[:, k + i : k + i + 1], (n, width)) for i in range(group)]
        ms, rows = [], []
        for i in range(group):
            at = k + i
            keep = sub > at if below_only else sub != at
            row = both[at : at + 1]
            for m, earlier in zip(ms, rows):
                row = row - m[at : at + 1] * earlier
            m = jnp.where(keep, cols[i] * (1.0 / cols[i][at : at + 1]), 0.0)
            for j in range(i + 1, group):
                cols[j] = cols[j] - m * cols[j][at : at + 1]
            ms.append(m)
            rows.append(row)
        for m, row in zip(ms, rows):
            both = both - m * row
    return both


def with_identity(matrix):
    n = matrix.shape[0]
    eye = iota((n, n), 0) == iota((n, n), 1)
    return jnp.concatenate([matrix, eye.astype(F32)], axis=1), eye


def inverse(matrix):
    n = matrix.shape[0]
    both, eye = with_identity(matrix)
    if n <= 64:
        both = eliminate(both, n, False)
    else:
        sub, lane = iota((n, 2 * n), 0), iota((n, 2 * n), 1)

        def step(k, both):
            row = jnp.sum(jnp.where(sub == k, both, 0.0), axis=0, keepdims=True)
            col = jnp.sum(jnp.where(lane == k, both, 0.0), axis=1, keepdims=True)
            piv = jnp.sum(jnp.where(lane[:1] == k, row, 0.0), axis=1, keepdims=True)
            return jnp.where(sub == k, row, both - col * (row / piv))

        both = lax.fori_loop(0, n, step, both)
    pivots = jnp.sum(jnp.where(eye, both[:, :n], 0.0), axis=1, keepdims=True)
    return both[:, n:] / pivots


def inverse_factor(matrix):
    n = matrix.shape[0]
    both, eye = with_identity(matrix)
    both = eliminate(both, n, True)
    pivots = jnp.sum(jnp.where(eye, both[:, :n], 0.0), axis=1, keepdims=True)
    return both[:, n:] / jnp.sqrt(pivots)


def kernel(
    n_rows,
    n_vec,
    self_hbm,
    link_hbm,
    links_hbm,
    coarse_hbm,
    vec_hbm,
    dir_hbm,
    res_ref,
    cor_ref,
    proj_ref,
    links_s,
    coarse_s,
    links_v,
    coarse_v,
    self_t,
    link_t,
    xp,
    wall,
    fin,
    win1,
    win2,
    win3,
    b_gx,
    b_cross,
    b_rhs,
    b_gb,
    b_ga,
    basis,
    deg,
    isq,
    dsh,
    rs,
    img,
    oht,
    first_r,
    rone_r,
    imw,
    load_sem,
    small_sem,
    halo_send,
    halo_recv,
    row_send,
    row_recv,
    vec_send,
    vec_recv,
):
    r = lax.axis_index("rows")
    v = lax.axis_index("vec")
    bc, bs = self_t.shape[0], self_t.shape[1]
    slots = link_t.shape[1]
    vc, slab = xp.shape[2:]
    kk = vc * n_vec
    nb = links_v.shape[1]
    nc = nb // 2
    lanes = b_gx.shape[2]

    small = [
        pltpu.make_async_copy(vec_hbm, xp.at[v, 0], small_sem.at[0]),
        pltpu.make_async_copy(dir_hbm, xp.at[v, 1], small_sem.at[1]),
        pltpu.make_async_copy(links_hbm, links_s, small_sem.at[2]),
        pltpu.make_async_copy(links_hbm, links_v, small_sem.at[3]),
        pltpu.make_async_copy(coarse_hbm, coarse_s, small_sem.at[4]),
        pltpu.make_async_copy(coarse_hbm, coarse_v, small_sem.at[5]),
    ]
    for load in small:
        load.start()

    def load_block(b):
        return (
            pltpu.make_async_copy(self_hbm.at[b], self_t.at[b], load_sem.at[0, b]),
            pltpu.make_async_copy(link_hbm.at[b], link_t.at[b], load_sem.at[1, b]),
        )

    for b in range(bc):
        for load in load_block(b):
            load.start()

    barrier = pltpu.get_barrier_semaphore()

    def greet_rows(off, c):
        pl.semaphore_signal(
            barrier, inc=1, device_id={"rows": lax.rem(r + off, n_rows)}, device_id_type=MESH
        )
        return c

    def greet_vec(off, c):
        pl.semaphore_signal(
            barrier, inc=1, device_id={"vec": lax.rem(v + off, n_vec)}, device_id_type=MESH
        )
        return c

    lax.fori_loop(1, n_rows, greet_rows, 0, unroll=n_rows <= 16)
    lax.fori_loop(1, n_vec, greet_vec, 0, unroll=n_vec <= 16)

    def over(axis, e, buf, what):
        mine, count = (r, n_rows) if axis == "rows" else (v, n_vec)
        ssem, rsem = (row_send, row_recv) if axis == "rows" else (vec_send, vec_recv)

        def one(off, c):
            other = lax.rem(mine + off, count)
            slot = other if what == "recv" else mine
            copy = pltpu.make_async_remote_copy(
                src_ref=buf.at[slot],
                dst_ref=buf.at[slot],
                send_sem=ssem.at[e, other],
                recv_sem=rsem.at[e, slot],
                device_id={axis: other},
                device_id_type=MESH,
            )
            if what == "start":
                copy.start()
            elif what == "recv":
                copy.wait_recv()
            else:
                copy.wait_send()
            return c

        lax.fori_loop(1, count, one, 0, unroll=count <= 16)

    def halo(e, win, what):
        def copy(direction):
            return pltpu.make_async_remote_copy(
                src_ref=win.at[pl.ds(bc, bc)],
                dst_ref=win.at[pl.ds(0 if direction == 0 else 2 * bc, bc)],
                send_sem=halo_send.at[e, direction],
                recv_sem=halo_recv.at[e, direction],
                device_id={
                    "rows": lax.rem(r + (1 if direction == 0 else n_rows - 1), n_rows)
                },
                device_id_type=MESH,
            )

        has_next = r < n_rows - 1
        has_prev = r > 0
        for direction in range(2):
            sends = has_next if direction == 0 else has_prev
            gets = has_prev if direction == 0 else has_next
            if what == "start":
                pl.when(sends)(lambda d=direction: copy(d).start())
            elif what == "recv":
                pl.when(gets)(lambda d=direction: copy(d).wait_recv())
            else:
                pl.when(sends)(lambda d=direction: copy(d).wait_send())

    def blocks(body):
        def step(b, c):
            body(b, pl.ds(pl.multiple_of(b * bs, bs), bs))
            return c

        lax.fori_loop(0, bc, step, 0, unroll=True)

    small[0].wait()
    small[1].wait()
    pl.semaphore_wait(barrier, n_rows + n_vec - 2)
    over("vec", EX_XP, xp, "start")

    base = r * bc
    tiles = (slots + 1) * bc
    total = jnp.zeros((bs, tiles), F32)
    tile_row = iota((tiles, bs), 0)
    for b in range(bc):
        for load in load_block(b):
            load.wait()
        for s in range(slots + 1):
            tile = self_t[b] if s == 0 else link_t[b, s - 1]
            one = jnp.where(tile_row == s * bc + b, 1.0, 0.0).astype(jnp.bfloat16)
            total = total + tile_dot(tile, one)
    rs[...] = total.T
    degree = rs[0:bc]
    for s in range(1, slots + 1):
        degree = degree + rs[s * bc : (s + 1) * bc]
    root = jnp.sqrt(degree)
    inv_root = 1.0 / root
    for b in range(bc):
        at = slice(b * bs, (b + 1) * bs)
        inv = jnp.broadcast_to(inv_root[b : b + 1], (8, bs))
        deg[:, at] = jnp.broadcast_to(root[b : b + 1], (8, bs))
        isq[:, at] = inv
        win1[bc + b, 0:vc] = xp[v, 0, :, at] * inv[0:vc]
        win1[bc + b, vc : 2 * vc] = xp[v, 1, :, at] * inv[0:vc]

    halo(0, win1, "start")

    lane8 = iota((bc, lanes), 1)
    tile_sums = jnp.zeros((bc, lanes), F32)
    block_degree = jnp.zeros((bc, 1), F32)
    for s in range(slots + 1):
        part = jnp.sum(rs[s * bc : (s + 1) * bc], axis=1, keepdims=True)
        block_degree = block_degree + part
        tile_sums = jnp.where(lane8 == s, part, tile_sums)
    tile_sums = jnp.where(lane8 == slots + 1, block_degree, tile_sums)
    b_gx[r, pl.ds(kk, bc), :] = tile_sums

    def self_part(win):
        total = jnp.zeros((bs, 8 * bc), F32)
        for b in range(bc):
            total = total + tile_dot(self_t[b], in_slot(win[bc + b], b, bc))
        return total

    def links_part(win, total):
        for b in range(bc):
            for s in range(slots):
                place = links_s[s, base + b] - base + bc
                remote = win[jnp.minimum(jnp.maximum(place, 0), 3 * bc - 1)]
                total = total + tile_dot(link_t[b, s], in_slot(remote, b, bc))
        return total.T

    image1 = self_part(win1)

    def diagonal_block(b, at):
        half = 128
        eye = iota((half, half), 0) == iota((half, half), 1)
        parts = []
        for h in range(bs // half):
            cut = self_t[b, h * half : (h + 1) * half, h * half : (h + 1) * half].astype(F32)
            parts.append(jnp.sum(jnp.where(eye, cut, 0.0), axis=0, keepdims=True))
        diag = jnp.concatenate(parts, axis=1)
        inv = isq[:, at]
        dsh[:, at] = damping / (1.0 + spectral_shift - diag * inv * inv)

    blocks(diagonal_block)

    for load in small[2:]:
        load.wait()
    lane_nc = iota((1, nc), 1)
    for s in range(slots + 1):
        for b in range(bc):
            target = base + b if s == 0 else links_s[s - 1, base + b]
            oht[s * bc + b : s * bc + b + 1, :] = (lane_nc == coarse_s[0, target]).astype(F32)

    over("vec", EX_XP, xp, "recv")
    for j in range(n_vec):
        basis[j * vc : (j + 1) * vc, :] = xp[j, 0]
        basis[2 * kk + j * vc : 2 * kk + (j + 1) * vc, :] = xp[j, 1]
    x_all = basis[0:kk, :]
    b_gx[r, 0:kk, 0:kk] = dot_nt(x_all, x_all)
    over("rows", EX_GRAM_X, b_gx, "start")

    halo(0, win1, "recv")
    image1 = links_part(win1, image1)
    for b in range(bc):
        at = slice(b * bs, (b + 1) * bs)
        adj = image1[8 * b : 8 * b + 8] * isq[:, at]
        img[0:vc, at] = xp[v, 0, :, at] - adj[0:vc]
        img[vc : 2 * vc, at] = xp[v, 1, :, at] - adj[vc : 2 * vc]
    b_cross[r, 0:vc, 0:kk] = dot_nt(img[0:vc, :], basis[0:kk, :])
    over("rows", EX_CROSS, b_cross, "start")

    over("rows", EX_GRAM_X, b_gx, "recv")
    got = jnp.sum(b_gx[:, 0:kk, 0:kk], axis=0)
    gram_inv = inverse(got)

    pick_sums = (iota((8, lanes), 0) == iota((8, lanes), 1)).astype(F32)
    sums = b_gx[:, kk : kk + bc, :].reshape(nb, lanes)
    sums_t = dot_nt(pick_sums, sums)
    sub_b, lane_b = iota((nb, nb), 0), iota((nb, nb), 1)
    by_block = jnp.where(sub_b == lane_b, sums_t[0:1], 0.0)
    for s in range(slots):
        by_block = by_block + jnp.where(links_v[s : s + 1] == sub_b, sums_t[s + 1 : s + 2], 0.0)
    pick = (iota((nc, nb), 0) == coarse_v[...]).astype(F32)
    tile_sum = dot_nt(dot_nt(pick, by_block), pick)
    agg = jnp.sum(pick * sums_t[slots + 1 : slots + 2], axis=1, keepdims=True)
    eye_c = iota((nc, nc), 0) == iota((nc, nc), 1)
    coarse = jnp.where(eye_c, (1.0 + spectral_shift) * agg, 0.0) - tile_sum
    to_gain = dot_nt(inverse(coarse), oht[...])

    over("rows", EX_CROSS, b_cross, "recv")
    cross_t = jnp.sum(b_cross[:, :, 0:kk], axis=0)
    coef_t = dot_nn(cross_t, gram_inv)
    residual = img[0:vc, :] - dot_nn(coef_t, basis[0:kk, :])[0:vc]
    res_ref[...] = residual
    first = residual * dsh[0:vc, :]
    first_r[...] = first

    def put2(b, at):
        win2[bc + b] = first_r[:, at] * isq[0:vc, at]

    blocks(put2)
    halo(1, win2, "start")

    image2 = self_part(win2)

    halo(1, win2, "recv")
    image2 = links_part(win2, image2)
    for b in range(bc):
        imw[:, b * bs : (b + 1) * bs] = image2[8 * b : 8 * b + vc]
    first = first_r[...]
    r_one = res_ref[...] - (1.0 + spectral_shift) * first + imw[...] * isq[0:vc, :]
    rone_r[...] = r_one
    weighted = r_one * deg[0:vc, :]
    rhs = jnp.zeros((vc, nc), F32)
    for b in range(bc):
        part = jnp.sum(weighted[:, b * bs : (b + 1) * bs], axis=1, keepdims=True)
        rhs = rhs + part * oht[b : b + 1, :]
    b_rhs[r, 0:vc, 0:nc] = rhs
    over("rows", EX_RHS, b_rhs, "start")
    over("rows", EX_RHS, b_rhs, "recv")
    gain = dot_nn(jnp.sum(b_rhs[:, :, 0:nc], axis=0), to_gain)[0:vc]

    def lift(b, at):
        moved = jnp.zeros((vc, bs), F32)
        for s in range(slots + 1):
            moved = moved + gain_at(s, b) * rs[s * bc + b : s * bc + b + 1]
        inv = isq[0:vc, at]
        lifted = deg[0:vc, at] * gain_at(0, b)
        rest = rone_r[:, at] - (1.0 + spectral_shift) * lifted + moved * inv
        out = first_r[:, at] + lifted + rest * dsh[0:vc, at]
        cor_ref[:, at] = out
        win3[bc + b] = out * inv

    def gain_at(s, b):
        return gain[:, s * bc + b : s * bc + b + 1]

    for b in range(bc):
        lift(b, pl.ds(b * bs, bs))
    halo(2, win3, "start")
    wall[v] = cor_ref[...]
    over("vec", EX_W, wall, "start")

    image3 = self_part(win3)

    over("vec", EX_W, wall, "recv")
    for j in range(n_vec):
        basis[kk + j * vc : kk + (j + 1) * vc, :] = wall[j]
    b_gb[r, :, 0 : 3 * kk] = dot_nt(basis[...], basis[...])
    over("rows", EX_GRAM_B, b_gb, "start")

    b_ga[r, 0 : 2 * vc, 0 : 3 * kk] = dot_nt(img[...], basis[...])
    halo(2, win3, "recv")
    image3 = links_part(win3, image3)
    for b in range(bc):
        imw[:, b * bs : (b + 1) * bs] = image3[8 * b : 8 * b + vc]
    imw[...] = cor_ref[...] - imw[...] * isq[0:vc, :]
    b_ga[r, 2 * vc : 3 * vc, 0 : 3 * kk] = dot_nt(imw[...], basis[...])
    over("rows", EX_GRAM_A, b_ga, "start")

    over("rows", EX_GRAM_B, b_gb, "recv")
    linv = inverse_factor(jnp.sum(b_gb[:, :, 0 : 3 * kk], axis=0))

    over("rows", EX_GRAM_A, b_ga, "recv")
    gram_a_t = jnp.sum(b_ga[:, :, 0 : 3 * kk], axis=0)
    fin[v, :, 0 : 3 * kk] = dot_nt(gram_a_t, linv)
    over("vec", EX_FINAL, fin, "start")
    over("vec", EX_FINAL, fin, "recv")
    parts = (
        [fin[j, 0:vc, 0 : 3 * kk] for j in range(n_vec)]
        + [fin[j, 2 * vc : 3 * vc, 0 : 3 * kk] for j in range(n_vec)]
        + [fin[j, vc : 2 * vc, 0 : 3 * kk] for j in range(n_vec)]
    )
    for j, part in enumerate(parts):
        basis[j * vc : (j + 1) * vc, 0 : 3 * kk] = part
    reduced = dot_nn(linv, basis[:, 0 : 3 * kk])
    proj_ref[...] = 0.5 * (reduced + reduced.T)

    over("vec", EX_XP, xp, "sent")
    over("vec", EX_W, wall, "sent")
    over("vec", EX_FINAL, fin, "sent")
    over("rows", EX_GRAM_X, b_gx, "sent")
    over("rows", EX_CROSS, b_cross, "sent")
    over("rows", EX_RHS, b_rhs, "sent")
    over("rows", EX_GRAM_B, b_gb, "sent")
    over("rows", EX_GRAM_A, b_ga, "sent")
    halo(0, win1, "sent")
    halo(1, win2, "sent")
    halo(2, win3, "sent")


def body(n_rows, n_vec, self_tiles, link_tiles, links, coarse_row, vectors, directions):
    bc, bs = self_tiles.shape[:2]
    slots = link_tiles.shape[1]
    vc, slab = vectors.shape
    nb = links.shape[0]
    nc = nb // 2
    kk = vc * n_vec

    def up(x, m):
        return -(-x // m) * m

    lanes = 128
    basis_lanes = up(3 * kk, 128)
    vm = functools.partial(pl.BlockSpec, memory_space=pltpu.VMEM)
    scratch = [
        pltpu.SMEM((slots, nb), jnp.int32),
        pltpu.SMEM((1, nb), jnp.int32),
        pltpu.VMEM((slots, nb), jnp.int32),
        pltpu.VMEM((1, nb), jnp.int32),
        pltpu.VMEM((bc, bs, bs), jnp.bfloat16),
        pltpu.VMEM((bc, slots, bs, bs), jnp.bfloat16),
        pltpu.VMEM((n_vec, 2, vc, slab), F32),
        pltpu.VMEM((n_vec, vc, slab), F32),
        pltpu.VMEM((n_vec, up(3 * vc, 8), basis_lanes), F32),
        pltpu.VMEM((3 * bc, 2 * vc, bs), F32),
        pltpu.VMEM((3 * bc, vc, bs), F32),
        pltpu.VMEM((3 * bc, vc, bs), F32),
        pltpu.VMEM((n_rows, kk + bc, lanes), F32),
        pltpu.VMEM((n_rows, up(vc, 8), up(kk, 128)), F32),
        pltpu.VMEM((n_rows, up(vc, 8), up(nc, 128)), F32),
        pltpu.VMEM((n_rows, 3 * kk, basis_lanes), F32),
        pltpu.VMEM((n_rows, up(3 * vc, 8), basis_lanes), F32),
        pltpu.VMEM((3 * kk, slab), F32),
        pltpu.VMEM((8, slab), F32),
        pltpu.VMEM((8, slab), F32),
        pltpu.VMEM((8, slab), F32),
        pltpu.VMEM(((slots + 1) * bc, bs), F32),
        pltpu.VMEM((2 * vc, slab), F32),
        pltpu.VMEM(((slots + 1) * bc, nc), F32),
        pltpu.VMEM((vc, slab), F32),
        pltpu.VMEM((vc, slab), F32),
        pltpu.VMEM((vc, slab), F32),
        pltpu.SemaphoreType.DMA((2, bc)),
        pltpu.SemaphoreType.DMA((6,)),
        pltpu.SemaphoreType.DMA((3, 2)),
        pltpu.SemaphoreType.DMA((3, 2)),
        pltpu.SemaphoreType.DMA((5, n_rows)),
        pltpu.SemaphoreType.DMA((5, n_rows)),
        pltpu.SemaphoreType.DMA((3, n_vec)),
        pltpu.SemaphoreType.DMA((3, n_vec)),
    ]
    return pl.pallas_call(
        functools.partial(kernel, n_rows, n_vec),
        out_shape=(
            jax.ShapeDtypeStruct((vc, slab), F32),
            jax.ShapeDtypeStruct((vc, slab), F32),
            jax.ShapeDtypeStruct((3 * kk, 3 * kk), F32),
        ),
        in_specs=[pl.BlockSpec(memory_space=pltpu.HBM)] * 6,
        out_specs=(vm(), vm(), vm()),
        scratch_shapes=scratch,
        compiler_params=pltpu.CompilerParams(
            collective_id=0, has_side_effects=True, vmem_limit_bytes=63 * 1024 * 1024
        ),
    )(
        self_tiles,
        link_tiles,
        links.T,
        coarse_row.reshape(1, nb),
        vectors,
        directions,
    )


def solution(mesh):
    in_specs = (
        P("rows", None, None),
        P("rows", None, None, None),
        P(),
        P(),
        P("vec", "rows"),
        P("vec", "rows"),
    )
    out_specs = (P("vec", "rows"), P("vec", "rows"), P())
    return jax.shard_map(
        functools.partial(body, mesh.shape["rows"], mesh.shape["vec"]),
        mesh=mesh,
        in_specs=in_specs,
        out_specs=out_specs,
        check_vma=False,
    )
```

profile of v0, /device:TPU:0, one launch (start us, length us, event | category | flops | bytes accessed | tf_op | source)
XLA Modules:
  0.0 49.5 jit_solution(11737900173246755405)
XLA Ops:
  0.6 44.7 %shard_map.85 = (f32[4,2048]{1,0:T(4,128)}, f32[4,2048]{1,0:T(4,128)}, f32[48,48]{1,0:T(8,128)}) custom-call(bf16[8,256,256]{2,1,0:T(8,128)(2,1)} %self_hbm.1, bf16[8,3,256,256]{3,2,1,0:T(8,128)(2,1)} %link_hbm.1, s32[3,64]{1,0:T(4,128)} %bitcast.2, s32[1,64]{1,0:T(1,128)} %bitcast.3, f32[4,2048]{1,0:T(4,128)} %vec_hbm.1, f32[4,2048]{1,0:T(4,128)} %dir_hbm.1), custom_call_target="tpu_custom_call" | custom-call | tf_op jit(solution)/shard_map/pallas_call | solution.py:523
  45.4 1.4 %copy.12 = f32[4,2048]{1,0:T(4,128)} copy(f32[4,2048]{1,0:T(4,128)} %get-tuple-element.6) | data formatting | bytes 65536
  46.7 1.4 %copy.13 = f32[4,2048]{1,0:T(4,128)} copy(f32[4,2048]{1,0:T(4,128)} %get-tuple-element.7) | data formatting | bytes 65536
  48.1 1.3 %copy.14 = f32[48,48]{1,0:T(8,128)} copy(f32[48,48]{1,0:T(8,128)} %get-tuple-element.8) | data formatting | bytes 18432
where the time goes:
time: 50 us; the launch traced here: 49.5 us
  Pallas kernels  44.7 us (89%)
  local copies, waits for them, and re-layouts  4.09 us (8%)
  between operations  0.64 us (1%)
    pallas_call x1, Pallas kernels, body(): pl.pallas_call(functools.partial(kernel, n_rows, n_vec), out_shape=(jax.S...  44.7 us
    unnamed x3, local copies, waits for them, and re-layouts  4.09 us

commit v1 on v0

--- a/solution.py
+++ b/solution.py
@@ -109,6 +109,9 @@
     coarse_hbm,
     vec_hbm,
     dir_hbm,
+    res_hbm,
+    cor_hbm,
+    proj_hbm,
     res_ref,
     cor_ref,
     proj_ref,
@@ -253,11 +256,6 @@
 
         lax.fori_loop(0, bc, step, 0, unroll=True)
 
-    small[0].wait()
-    small[1].wait()
-    pl.semaphore_wait(barrier, n_rows + n_vec - 2)
-    over("vec", EX_XP, xp, "start")
-
     base = r * bc
     tiles = (slots + 1) * bc
     total = jnp.zeros((bs, tiles), F32)
@@ -273,6 +271,8 @@
     degree = rs[0:bc]
     for s in range(1, slots + 1):
         degree = degree + rs[s * bc : (s + 1) * bc]
+    small[0].wait()
+    small[1].wait()
     root = jnp.sqrt(degree)
     inv_root = 1.0 / root
     for b in range(bc):
@@ -283,7 +283,9 @@
         win1[bc + b, 0:vc] = xp[v, 0, :, at] * inv[0:vc]
         win1[bc + b, vc : 2 * vc] = xp[v, 1, :, at] * inv[0:vc]
 
+    pl.semaphore_wait(barrier, n_rows + n_vec - 2)
     halo(0, win1, "start")
+    over("vec", EX_XP, xp, "start")
 
     lane8 = iota((bc, lanes), 1)
     tile_sums = jnp.zeros((bc, lanes), F32)
@@ -373,6 +375,8 @@
     coef_t = dot_nn(cross_t, gram_inv)
     residual = img[0:vc, :] - dot_nn(coef_t, basis[0:kk, :])[0:vc]
     res_ref[...] = residual
+    out_res = pltpu.make_async_copy(res_ref, res_hbm, small_sem.at[6])
+    out_res.start()
     first = residual * dsh[0:vc, :]
     first_r[...] = first
 
@@ -381,6 +385,19 @@
 
     blocks(put2)
     halo(1, win2, "start")
+
+    rhs = jnp.zeros((vc, nc), F32)
+    direct = (res_ref[...] - (1.0 + spectral_shift) * first) * deg[0:vc, :]
+    for b in range(bc):
+        sent = win2[bc + b].astype(jnp.bfloat16).astype(F32)
+        for s in range(slots + 1):
+            t = s * bc + b
+            terms = sent * rs[t : t + 1]
+            if s == 0:
+                terms = terms + direct[:, b * bs : (b + 1) * bs]
+            rhs = rhs + jnp.sum(terms, axis=1, keepdims=True) * oht[t : t + 1, :]
+    b_rhs[r, 0:vc, 0:nc] = rhs
+    over("rows", EX_RHS, b_rhs, "start")
 
     image2 = self_part(win2)
 
@@ -391,13 +408,6 @@
     first = first_r[...]
     r_one = res_ref[...] - (1.0 + spectral_shift) * first + imw[...] * isq[0:vc, :]
     rone_r[...] = r_one
-    weighted = r_one * deg[0:vc, :]
-    rhs = jnp.zeros((vc, nc), F32)
-    for b in range(bc):
-        part = jnp.sum(weighted[:, b * bs : (b + 1) * bs], axis=1, keepdims=True)
-        rhs = rhs + part * oht[b : b + 1, :]
-    b_rhs[r, 0:vc, 0:nc] = rhs
-    over("rows", EX_RHS, b_rhs, "start")
     over("rows", EX_RHS, b_rhs, "recv")
     gain = dot_nn(jnp.sum(b_rhs[:, :, 0:nc], axis=0), to_gain)[0:vc]
 
@@ -418,6 +428,8 @@
     for b in range(bc):
         lift(b, pl.ds(b * bs, bs))
     halo(2, win3, "start")
+    out_cor = pltpu.make_async_copy(cor_ref, cor_hbm, small_sem.at[7])
+    out_cor.start()
     wall[v] = cor_ref[...]
     over("vec", EX_W, wall, "start")
 
@@ -455,6 +467,8 @@
         basis[j * vc : (j + 1) * vc, 0 : 3 * kk] = part
     reduced = dot_nn(linv, basis[:, 0 : 3 * kk])
     proj_ref[...] = 0.5 * (reduced + reduced.T)
+    out_proj = pltpu.make_async_copy(proj_ref, proj_hbm, small_sem.at[8])
+    out_proj.start()
 
     over("vec", EX_XP, xp, "sent")
     over("vec", EX_W, wall, "sent")
@@ -467,6 +481,9 @@
     halo(0, win1, "sent")
     halo(1, win2, "sent")
     halo(2, win3, "sent")
+    out_res.wait()
+    out_cor.wait()
+    out_proj.wait()
 
 
 def body(n_rows, n_vec, self_tiles, link_tiles, links, coarse_row, vectors, directions):
@@ -482,8 +499,11 @@
 
     lanes = 128
     basis_lanes = up(3 * kk, 128)
-    vm = functools.partial(pl.BlockSpec, memory_space=pltpu.VMEM)
+    hbm = pl.BlockSpec(memory_space=pltpu.HBM)
     scratch = [
+        pltpu.VMEM((vc, slab), F32),
+        pltpu.VMEM((vc, slab), F32),
+        pltpu.VMEM((3 * kk, 3 * kk), F32),
         pltpu.SMEM((slots, nb), jnp.int32),
         pltpu.SMEM((1, nb), jnp.int32),
         pltpu.VMEM((slots, nb), jnp.int32),
@@ -512,7 +532,7 @@
         pltpu.VMEM((vc, slab), F32),
         pltpu.VMEM((vc, slab), F32),
         pltpu.SemaphoreType.DMA((2, bc)),
-        pltpu.SemaphoreType.DMA((6,)),
+        pltpu.SemaphoreType.DMA((9,)),
         pltpu.SemaphoreType.DMA((3, 2)),
         pltpu.SemaphoreType.DMA((3, 2)),
         pltpu.SemaphoreType.DMA((5, n_rows)),
@@ -520,15 +540,16 @@
         pltpu.SemaphoreType.DMA((3, n_vec)),
         pltpu.SemaphoreType.DMA((3, n_vec)),
     ]
-    return pl.pallas_call(
+    out_shape = (
+        jax.ShapeDtypeStruct((vc, slab), F32),
+        jax.ShapeDtypeStruct((vc, slab), F32),
+        jax.ShapeDtypeStruct((3 * kk, 3 * kk), F32),
+    )
+    results = pl.pallas_call(
         functools.partial(kernel, n_rows, n_vec),
-        out_shape=(
-            jax.ShapeDtypeStruct((vc, slab), F32),
-            jax.ShapeDtypeStruct((vc, slab), F32),
-            jax.ShapeDtypeStruct((3 * kk, 3 * kk), F32),
-        ),
-        in_specs=[pl.BlockSpec(memory_space=pltpu.HBM)] * 6,
-        out_specs=(vm(), vm(), vm()),
+        out_shape=out_shape,
+        in_specs=[hbm] * 6,
+        out_specs=(hbm, hbm, hbm),
         scratch_shapes=scratch,
         compiler_params=pltpu.CompilerParams(
             collective_id=0, has_side_effects=True, vmem_limit_bytes=63 * 1024 * 1024
@@ -541,6 +562,26 @@
         vectors,
         directions,
     )
+    return pl.pallas_call(
+        hand_over,
+        out_shape=out_shape,
+        in_specs=[hbm] * 3,
+        out_specs=(hbm, hbm, hbm),
+        scratch_shapes=[pltpu.SemaphoreType.DMA((3,))],
+        compiler_params=pltpu.CompilerParams(vmem_limit_bytes=63 * 1024 * 1024),
+    )(*results)
+
+
+def hand_over(a, b, c, out_a, out_b, out_c, sem):
+    copies = [
+        pltpu.make_async_copy(a, out_a, sem.at[0]),
+        pltpu.make_async_copy(b, out_b, sem.at[1]),
+        pltpu.make_async_copy(c, out_c, sem.at[2]),
+    ]
+    for copy in copies:
+        copy.start()
+    for copy in copies:
+        copy.wait()
 
 
 def solution(mesh):

time: 50 us -> 45.7 us (0.914)
  local copies, waits for them, and re-layouts: 4.09 us -> 0 us
    unnamed x3 -> x0, local copies, waits for them, and re-layouts: 4.09 us -> none
    pallas_call x1 -> x2, Pallas kernels: 44.7 us -> 44.9 us  [the longest x1 41 us: body(): pl.pallas_call(functools.partial(kernel, n_rows, n_vec), out_shape=out_sh...]
where the time goes in v1:
time: 45.7 us; the launch traced here: 45.5 us
  Pallas kernels  44.9 us (98%)
  between operations  0.64 us (1%)
    pallas_call x1, Pallas kernels, body(): pl.pallas_call(functools.partial(kernel, n_rows, n_vec), out_shape=out_sh...  41 us
    pallas_call x1, Pallas kernels, body(): pl.pallas_call(hand_over, out_shape=out_shape, in_specs=[hbm] * 3, out_sp...  3.86 us

profile of v1, /device:TPU:0, one launch (start us, length us, event | category | flops | bytes accessed | tf_op | source)
XLA Modules:
  0.0 45.5 jit_solution(10734496763304986527)
XLA Ops:
  0.6 41.0 %shard_map.85 = (f32[4,2048]{1,0:T(4,128)}, f32[4,2048]{1,0:T(4,128)}, f32[48,48]{1,0:T(8,128)}) custom-call(bf16[8,256,256]{2,1,0:T(8,128)(2,1)} %self_hbm.1, bf16[8,3,256,256]{3,2,1,0:T(8,128)(2,1)} %link_hbm.1, s32[3,64]{1,0:T(4,128)} %bitcast.2, s32[1,64]{1,0:T(1,128)} %bitcast.3, f32[4,2048]{1,0:T(4,128)} %vec_hbm.1, f32[4,2048]{1,0:T(4,128)} %dir_hbm.1), custom_call_target="tpu_custom_call" | custom-call | tf_op jit(solution)/shard_map/pallas_call | solution.py:548
  41.7 3.9 %shard_map.86 = (f32[4,2048]{1,0:T(4,128)}, f32[4,2048]{1,0:T(4,128)}, f32[48,48]{1,0:T(8,128)}) custom-call(f32[4,2048]{1,0:T(4,128)} %get-tuple-element.6.a, f32[4,2048]{1,0:T(4,128)} %get-tuple-element.7.b, f32[48,48]{1,0:T(8,128)} %get-tuple-element.8.c), custom_call_target="tpu_custom_call" | custom-call | tf_op jit(solution)/shard_map/pallas_call | solution.py:565

commit v2 on v1

--- a/solution.py
+++ b/solution.py
@@ -567,20 +567,22 @@
         out_shape=out_shape,
         in_specs=[hbm] * 3,
         out_specs=(hbm, hbm, hbm),
-        scratch_shapes=[pltpu.SemaphoreType.DMA((3,))],
+        scratch_shapes=[pltpu.VMEM(o.shape, F32) for o in out_shape]
+        + [pltpu.SemaphoreType.DMA((2, 3))],
         compiler_params=pltpu.CompilerParams(vmem_limit_bytes=63 * 1024 * 1024),
     )(*results)
 
 
-def hand_over(a, b, c, out_a, out_b, out_c, sem):
-    copies = [
-        pltpu.make_async_copy(a, out_a, sem.at[0]),
-        pltpu.make_async_copy(b, out_b, sem.at[1]),
-        pltpu.make_async_copy(c, out_c, sem.at[2]),
-    ]
-    for copy in copies:
+def hand_over(a, b, c, out_a, out_b, out_c, held_a, held_b, held_c, sem):
+    refs = ((a, held_a, out_a), (b, held_b, out_b), (c, held_c, out_c))
+    gets = [pltpu.make_async_copy(x, h, sem.at[0, i]) for i, (x, h, _) in enumerate(refs)]
+    puts = [pltpu.make_async_copy(h, y, sem.at[1, i]) for i, (_, h, y) in enumerate(refs)]
+    for copy in gets:
         copy.start()
-    for copy in copies:
+    for get, put in zip(gets, puts):
+        get.wait()
+        put.start()
+    for copy in puts:
         copy.wait()
 
 

time: 45.7 us -> 43.3 us (0.947)
  Pallas kernels: 44.9 us -> 42.5 us
    pallas_call x1, Pallas kernels: 3.86 us -> 1.45 us  [body(): pl.pallas_call(hand_over, out_shape=out_shape, in_specs=[hbm] * 3, out_sp...]
where the time goes in v2:
time: 43.3 us; the launch traced here: 43.1 us
  Pallas kernels  42.5 us (98%)
  between operations  0.64 us (1%)
    pallas_call x1, Pallas kernels, body(): pl.pallas_call(functools.partial(kernel, n_rows, n_vec), out_shape=out_sh...  41 us
    pallas_call x1, Pallas kernels, body(): pl.pallas_call(hand_over, out_shape=out_shape, in_specs=[hbm] * 3, out_sp...  1.45 us

profile of v2, /device:TPU:0, one launch (start us, length us, event | category | flops | bytes accessed | tf_op | source)
XLA Modules:
  0.0 43.1 jit_solution(17905093506383338698)
XLA Ops:
  0.6 41.0 %shard_map.85 = (f32[4,2048]{1,0:T(4,128)}, f32[4,2048]{1,0:T(4,128)}, f32[48,48]{1,0:T(8,128)}) custom-call(bf16[8,256,256]{2,1,0:T(8,128)(2,1)} %self_hbm.1, bf16[8,3,256,256]{3,2,1,0:T(8,128)(2,1)} %link_hbm.1, s32[3,64]{1,0:T(4,128)} %bitcast.2, s32[1,64]{1,0:T(1,128)} %bitcast.3, f32[4,2048]{1,0:T(4,128)} %vec_hbm.1, f32[4,2048]{1,0:T(4,128)} %dir_hbm.1), custom_call_target="tpu_custom_call" | custom-call | tf_op jit(solution)/shard_map/pallas_call | solution.py:548
  41.7 1.4 %shard_map.86 = (f32[4,2048]{1,0:T(4,128)}, f32[4,2048]{1,0:T(4,128)}, f32[48,48]{1,0:T(8,128)}) custom-call(f32[4,2048]{1,0:T(4,128)} %get-tuple-element.6.a, f32[4,2048]{1,0:T(4,128)} %get-tuple-element.7.b, f32[48,48]{1,0:T(8,128)} %get-tuple-element.8.c), custom_call_target="tpu_custom_call" | custom-call | tf_op jit(solution)/shard_map/pallas_call | solution.py:565
